TPU v7x, 256 devices: a whole 4x4x8 slice. The times are simulated.
256 devices in a mesh: rep: 2 (over core), expert: 128 (over y, z, x).
Axes of the slice: x: 4, y: 4, z: 8, core: 2. Of those that a mesh axis runs over, the one named last changes fastest.
Arguments:
- tokens: bfloat16 [2048, 3584], P('expert'), may hold values from -6 to 6
- expert_ids: int32 [2048, 8], P('expert'), may hold values from 0 to 127, all different within a row; in each aligned block of 16 rows (0 to 15, 16 to 31, ...) at most 2 rows name the same one
- gate_scores: float32 [2048, 8], P('expert'), may hold values from 0.05 to 1
- w_gate: bfloat16 [128, 3584, 1024], P('expert', None, 'rep'), may hold values from -0.09375 to 0.09375
- w_up: bfloat16 [128, 3584, 1024], P('expert', None, 'rep'), may hold values from -0.09375 to 0.09375
- w_down: bfloat16 [128, 1024, 3584], P('expert', 'rep'), may hold values from -0.1875 to 0.1875
Outputs:
- combined: bfloat16 [2048, 3584], P('expert', 'rep')
Inputs may be any that keep to these rules, and one draw needn't show every extreme that they name: `expert_ids`: each row names 8 different experts; within the rows of one device no expert is named by more than 2 rows, a bound that some block reaches.
All inputs are finite; a program needn't handle non-finite values.
Results may differ from a plain program's by a relative error of at most 0.0057.
Values may be sent and summed in bfloat16 or wider, within the bound.
A program may use at most 64 MiB of HBM per device.

v0:
```python
import jax
import jax.numpy as jnp
from jax import lax
from jax.sharding import PartitionSpec as P


def expert_rows(block_rows, gate_weight, up_weight, down_weight):
    gate_proj = jnp.dot(block_rows, gate_weight, preferred_element_type=jnp.float32)
    up_proj = jnp.dot(block_rows, up_weight, preferred_element_type=jnp.float32)
    hidden = (jax.nn.silu(gate_proj) * up_proj).astype(jnp.bfloat16)
    return jnp.dot(hidden, down_weight, preferred_element_type=jnp.float32)


def shards(tokens, expert_ids, gate_scores, w_gate, w_up, w_down):
    devices = lax.axis_size("expert")
    tok_rows = tokens.shape[0]
    model_width = tokens.shape[1]
    top_count = expert_ids.shape[1]
    capacity = max(2, 2 * tok_rows * top_count // devices)
    flat_ids = expert_ids.reshape(-1)
    one_hot = (flat_ids[:, None] == jnp.arange(devices, dtype=jnp.int32)[None, :]).astype(jnp.int32)
    row_rank = jnp.sum(jnp.cumsum(one_hot, 0) * one_hot, 1) - 1
    position = flat_ids * capacity + row_rank
    token_index = jnp.arange(flat_ids.shape[0], dtype=jnp.int32) // top_count
    send_rows = (
        jnp.zeros((devices * capacity, model_width), jnp.bfloat16)
        .at[position]
        .set(tokens[token_index])
    )
    arrived = lax.all_to_all(
        send_rows.reshape(devices, capacity, model_width),
        "expert",
        split_axis=0,
        concat_axis=0,
        tiled=True,
    )
    partial_value = expert_rows(arrived.reshape(-1, model_width), w_gate[0], w_up[0], w_down[0])
    partial_value = partial_value.reshape(devices, capacity, model_width)
    expert_out = lax.psum_scatter(partial_value, "rep", scatter_dimension=2, tiled=True).astype(
        jnp.bfloat16
    )
    returned = lax.all_to_all(expert_out, "expert", split_axis=0, concat_axis=0, tiled=True)
    picked = returned.reshape(devices * capacity, model_width // 2)[position]
    weighted = picked.astype(jnp.float32) * gate_scores.reshape(-1)[:, None]
    combined = jnp.sum(weighted.reshape(tok_rows, top_count, model_width // 2), 1)
    return combined.astype(jnp.bfloat16)


def solution(mesh):
    in_specs = (
        P("expert", None),
        P("expert", None),
        P("expert", None),
        P("expert", None, "rep"),
        P("expert", None, "rep"),
        P("expert", "rep", None),
    )
    out_specs = P("expert", "rep")
    return jax.shard_map(shards, mesh=mesh, in_specs=in_specs, out_specs=out_specs, check_vma=False)
```

profile of v0, /device:TPU:32, one launch (start us, length us, event | category | flops | bytes accessed | tf_op | source)
XLA Modules:
  0.0 160.1 jit_solution(9925588093687756852)
XLA Ops:
  6.5 0.0 copy-start
  6.5 0.0 reduce-scatter.2.cloned.1.call-start
  6.5 0.8 copy.17
  7.3 0.7 broadcast_multiply_fusion
  8.0 0.1 eq.15
  8.1 0.1 fusion.17
  8.2 0.2 reduce_window_sum.11
  8.4 0.2 select_reduce_fusion
  8.6 0.1 copy.16
  8.6 0.1 mul.37
  8.8 0.0 copy-done
  8.8 6.0 %scatter_custom_fusion = bf16[256,3584]{1,0:T(8,128)(2,1)} fusion(s32[128]{0:T(128)S(1)} %fusion.19, bf16[16,3584]{1,0:T(8,128)(2,1)S(1)} %copy-done, s32[1024]{0:T(1024)S(1)} %pad_clamp_fusion.1, bf16[]{:T(256)} %constant.28.clone.1), kind=kCustom, calls=%fused_computation.13 | custom fusion | bytes 1835010 | tf_op jit(solution)/shard_map/scatter | solution.py:28
  14.8 3.9 %reshape.99 = bf16[128,2,3584]{2,1,0:T(2,128)(2,1)S(1)} reshape(bf16[256,3584]{1,0:T(8,128)(2,1)} %scatter_custom_fusion) | data formatting | bytes 3670016 | tf_op jit(solution)/shard_map/reshape | solution.py:31
  18.7 61.7 %all_to_all.10 = bf16[128,2,3584]{2,1,0:T(2,128)(2,1)} all-to-all(bf16[128,2,3584]{2,1,0:T(2,128)(2,1)S(1)} %reshape.99), channel_id=1, replica_groups=mesh['rep'=2,'expert'=128] {'expert'}, dimensions={0} | all-to-all | bytes 3670016 | tf_op jit(solution)/shard_map/all_to_all | solution.py:30
  80.4 4.1 %reshape.100 = bf16[256,3584]{1,0:T(8,128)(2,1)S(1)} reshape(bf16[128,2,3584]{2,1,0:T(2,128)(2,1)} %all_to_all.10) | data formatting | bytes 3670016 | tf_op jit(solution)/shard_map/reshape | solution.py:37
  84.5 0.0 copy-start.2
  84.5 3.3 %fusion.4 = f32[256,512]{1,0:T(8,128)S(1)} fusion(bf16[256,3584]{1,0:T(8,128)(2,1)S(1)} %reshape.100, bf16[1,3584,512]{2,1,0:T(8,128)(2,1)} %param.9), kind=kOutput, calls=%fused_computation.7 | convolution fusion | flops 939524096 | bytes 6029312 | tf_op jit(solution)/shard_map/dot_general | solution.py:8
  87.8 0.0 copy-done.2
  87.8 1.1 fusion.9
  89.0 0.1 dot_general.13
  89.1 5.0 %fusion = f32[128,2,3584]{2,0,1:T(8,128)} fusion(bf16[1,512,3584]{2,1,0:T(8,128)(2,1)} %param.11, bf16[128,2,512]{2,1,0:T(2,128)(2,1)S(1)} %dot_general.13), kind=kOutput, calls=%fused_computation.3 | convolution fusion | flops 939524096 | bytes 7602176 | tf_op jit(solution)/shard_map/dot_general | solution.py:11
  94.0 0.0 reduce-scatter.2.cloned.1.call-update
  94.0 11.8 %reduce-scatter.2.cloned.1.call-done = f32[128,2,1792]{2,0,1:T(8,128)} async-done(((f32[128,2,3584]{2,0,1:T(8,128)}), f32[128,2,1792]{2,0,1:T(8,128)}) %reduce-scatter.2.cloned.1.call-update) | async-done | bytes 1835024 | tf_op jit(solution)/shard_map/reduce_scatter | solution.py:39
  105.8 1.6 convert_element_type.21
  107.4 0.0 copy-start.1
  107.5 1.9 %copy.19 = bf16[128,2,1792]{2,1,0:T(2,128)(2,1)} copy(bf16[128,2,1792]{2,0,1:T(8,128)(2,1)S(1)} %convert_element_type.21) | data formatting | bytes 1835008 | tf_op jit(solution)/shard_map/convert_element_type | solution.py:39
  109.3 13.7 %all-to-all-start.1 = ((bf16[128,2,1792]{2,1,0:T(2,128)(2,1)}), bf16[128,2,1792]{2,1,0:T(2,128)(2,1)S(1)}, u32[]{:S(2)}, u32[]{:S(2)}) async-start(bf16[128,2,1792]{2,1,0:T(2,128)(2,1)} %copy.19), calls=%async_computation.2 | async-start | bytes 1835008 | tf_op jit(solution)/shard_map/all_to_all | solution.py:42
  123.0 0.0 copy-done.1
  123.0 0.1 copy.20
  123.1 27.8 %all-to-all-done.1 = bf16[128,2,1792]{2,1,0:T(2,128)(2,1)S(1)} async-done(((bf16[128,2,1792]{2,1,0:T(2,128)(2,1)}), bf16[128,2,1792]{2,1,0:T(2,128)(2,1)S(1)}, u32[]{:S(2)}, u32[]{:S(2)}) %all-to-all-start.1) | async-done | bytes 917536 | tf_op jit(solution)/shard_map/all_to_all | solution.py:42
  150.9 0.3 reshape.101
  151.3 0.9 gather_fusion
  152.2 1.1 fusion.12
  (4 shorter events, 0.0 us)
Async XLA Ops:
  6.5 2.2 %copy-start = (bf16[16,3584]{1,0:T(8,128)(2,1)S(1)}, bf16[16,3584]{1,0:T(8,128)(2,1)}, u32[]{:S(2)}) copy-start(bf16[16,3584]{1,0:T(8,128)(2,1)} %param.6) | copy-start | bytes 344068
  6.5 99.3 %reduce-scatter.2.cloned.1.call-start = ((), (), s32[]{:S(2)}) async-start(), calls=%async_computation.3 | async-start | bytes 5505024 | tf_op jit(solution)/shard_map/reduce_scatter | solution.py:39
  84.5 3.3 %copy-start.2 = (bf16[1,3584,512]{2,1,0:T(8,128)(2,1)S(1)}, bf16[1,3584,512]{2,1,0:T(8,128)(2,1)}, u32[]{:S(2)}) copy-start(bf16[1,3584,512]{2,1,0:T(8,128)(2,1)} %param.10) | copy-start | bytes 11010052
  107.4 15.6 %copy-start.1 = (f32[16,8]{0,1:T(8,128)S(1)}, f32[16,8]{0,1:T(8,128)}, u32[]{:S(2)}) copy-start(f32[16,8]{0,1:T(8,128)} %param.8) | copy-start | bytes 1540
  109.3 41.6 %all-to-all-start.1 = ((bf16[128,2,1792]{2,1,0:T(2,128)(2,1)}), bf16[128,2,1792]{2,1,0:T(2,128)(2,1)S(1)}, u32[]{:S(2)}, u32[]{:S(2)}) async-start(bf16[128,2,1792]{2,1,0:T(2,128)(2,1)} %copy.19), calls=%async_computation.2 | async-start | bytes 1835008 | tf_op jit(solution)/shard_map/all_to_all | solution.py:42
Sparse Core Ops, SparseCore 0:
  94.2 11.6 reduce-scatter.1
where the time goes:
time: 160 us
  blocking collectives  61.7 us (39%)
  waiting for transfers between devices  39.7 us (25%)
  local copies, waits for them, and re-layouts  18.4 us (11%)
  starting transfers between devices  13.7 us (9%)
  between operations  13.5 us (8%)
  matrix products  9.38 us (6%)
  other arithmetic  3.79 us (2%)
    all_to_all x1, blocking collectives, shards(): lax.all_to_all(send_rows.reshape(devices, capacity, model_width), 'expert...  61.7 us
    all_to_all x1, waiting for transfers between devices, shards(): lax.all_to_all(expert_out, 'expert', split_axis=0, concat_axis=0, tiled=T...  27.8 us
    all_to_all x1, starting transfers between devices, shards(): lax.all_to_all(expert_out, 'expert', split_axis=0, concat_axis=0, tiled=T...  13.7 us
    reduce_scatter x1, waiting for transfers between devices, shards(): lax.psum_scatter(partial_value, 'rep', scatter_dimension=2, tiled=True)  11.8 us
    scatter x1, local copies, waits for them, and re-layouts, shards(): send_rows = jnp.zeros((devices * capacity, model_width), jnp.bfloat16).at...  6.05 us
    dot_general x1, matrix products, expert_rows(): return jnp.dot(hidden, down_weight, preferred_element_type=jnp.float32)  4.96 us
    reshape x1, local copies, waits for them, and re-layouts, shards(): arrived.reshape(-1, model_width)  4.06 us
    reshape x1, local copies, waits for them, and re-layouts, shards(): send_rows.reshape(devices, capacity, model_width)  3.88 us
  transfers between devices with their start and end apart: 2, of which 2 were waited for; matrix products, arithmetic and copies ran while one was open for 0% of the time, Pallas kernels for 0%

commit v1 on v0

v1 whole, which is shorter than its diff:
```python
import functools

import jax
import jax.numpy as jnp
from jax import lax
from jax.experimental import pallas as pl
from jax.experimental.pallas import tpu as pltpu
from jax.sharding import PartitionSpec as P

NX, NY, NZ = 4, 4, 8
ROWS = 16
TOP = 8
CAP = 2
HALF = 1792
HID = 512
SLOTS = NX * NY * NZ * CAP
COLUMN = NZ * ROWS
CHUNKS_IN = (256, 512, 512, 512)
CHUNKS_OUT = (512, 512, 512, 256)
BF = jnp.bfloat16
F32 = jnp.float32


def starts(widths):
    return [sum(widths[:i]) for i in range(len(widths))]


def dot(lhs, rhs):
    return jnp.dot(lhs, rhs, preferred_element_type=F32)


def kernel(tok, ids, sc, wg, wu, wd, out, *scratch):
    names = iter(scratch)
    n_in, n_out = len(CHUNKS_IN), len(CHUNKS_OUT)
    take = lambda n: [next(names) for _ in range(n)]
    zbuf, send, recv1, recv2, sib = (take(n_in) for _ in range(5))
    outb, ret1, ret2, zsend, zrecv, own = (take(n_out) for _ in range(6))
    ids_v, sc_v, meta, sel_t, w_hi, w_lo, hid, hid_sib, acc_g, acc_u = take(10)
    wg_v, wu_v, wd_own, wd_sib = take(4)
    local, send_sem, recv_sem = take(3)

    r = lax.axis_index("rep")
    e = lax.axis_index("expert")
    y, z, x = e // 32, (e // 4) % 8, e % 4
    a = x * (1 - r) + y * r
    b = y * (1 - r) + x * r

    def device(a_at, b_at, z_at, r_at=r):
        y_at = b_at * (1 - r) + a_at * r
        x_at = a_at * (1 - r) + b_at * r
        return {"rep": r_at, "expert": (y_at * 8 + z_at) * 4 + x_at}

    def along_a(step):
        return device((a + step + 4) % 4, b, z)

    def along_b(step):
        return device(a, (b + step + 4) % 4, z)

    def along_z(step):
        return device(a, b, (z + step + 8) % 8)

    sibling = device(a, b, z, 1 - r)

    index = {}

    def sem_of(key):
        return index.setdefault(key, len(index))

    def push(src, dst, key, target):
        at = sem_of(key)
        pltpu.make_async_remote_copy(
            src_ref=src,
            dst_ref=dst,
            send_sem=send_sem.at[at],
            recv_sem=recv_sem.at[at],
            device_id=target,
        ).start()

    def whole(ref, key):
        at = sem_of(key)
        return pltpu.make_async_remote_copy(
            src_ref=ref,
            dst_ref=ref,
            send_sem=send_sem.at[at],
            recv_sem=recv_sem.at[at],
            device_id=sibling,
        )

    sent = []

    def arrived(ref, key):
        whole(ref, key).wait_recv()
        sent.append((ref, key))

    in_at, out_at = starts(CHUNKS_IN), starts(CHUNKS_OUT)
    mine, other = r * HALF, (1 - r) * HALF

    loads = {}

    def load(name, src, dst):
        loads[name] = pltpu.make_async_copy(src, dst, local.at[len(loads)])
        loads[name].start()

    load("ids", ids, ids_v)
    load("sc", sc, sc_v)
    for c, width in enumerate(CHUNKS_IN):
        load(("tok", c), tok.at[:, pl.ds(pl.multiple_of(mine + in_at[c], 128), width)], zbuf[c].at[0])
    for half, base in ((0, mine), (1, other)):
        rows = pl.ds(pl.multiple_of(base, 128), HALF)
        load(("wg", half), wg.at[0, rows, :], wg_v.at[half])
        load(("wu", half), wu.at[0, rows, :], wu_v.at[half])
    load("wd", wd.at[0, :, pl.ds(pl.multiple_of(mine, 128), HALF)], wd_own)

    barrier = pltpu.get_barrier_semaphore()
    for step in range(1, NZ):
        pl.semaphore_signal(barrier, inc=1, device_id=along_z(step))
    for step in range(1, 4):
        pl.semaphore_signal(barrier, inc=1, device_id=along_a(step))
        pl.semaphore_signal(barrier, inc=1, device_id=along_b(step))
    pl.semaphore_signal(barrier, inc=1, device_id=sibling)

    loads["ids"].wait()
    loads["sc"].wait()
    meta[0, 0:ROWS, 0:TOP] = ids_v[...].astype(F32).T
    meta[0, ROWS:, 0:TOP] = sc_v[...].T
    for c in range(n_in):
        loads["tok", c].wait()
    pl.semaphore_wait(barrier, NZ - 1 + 3 + 3 + 1)

    for step in range(1, NZ):
        push(meta.at[0], meta.at[step], "meta", along_z(step))
    for c in range(n_in):
        for step in range(1, NZ):
            push(zbuf[c].at[0], zbuf[c].at[step], ("z", c), along_z(step))
    push(wd.at[0, :, pl.ds(pl.multiple_of(other, 128), HALF)], wd_sib, "wd", sibling)

    arrived(meta.at[pl.ds(1, NZ - 1)], "meta")
    lane = lax.broadcasted_iota(jnp.int32, (COLUMN, SLOTS), 1)
    row = lax.broadcasted_iota(jnp.int32, (COLUMN, SLOTS), 0)
    a_to = (a + (lane >> 6)) & 3
    b_to = (b + ((lane >> 4) & 3)) & 3
    y_to = b_to * (1 - r) + a_to * r
    x_to = a_to * (1 - r) + b_to * r
    named = ((y_to * 8 + z) * 4 + x_to).astype(F32)
    same = ((lane >> 1) & 7) == (row >> 4)
    ids_all = meta[:, 0:ROWS, :].reshape(COLUMN, 128)
    sc_all = meta[:, ROWS:, :].reshape(COLUMN, 128)
    member = jnp.zeros((COLUMN, SLOTS), F32)
    weight = jnp.zeros((COLUMN, SLOTS), F32)
    for k in range(TOP):
        hit = (ids_all[:, k : k + 1] == named) & same
        member = jnp.where(hit, 1.0, member)
        weight = jnp.where(hit, sc_all[:, k : k + 1], weight)
    to_row = lax.broadcasted_iota(jnp.int32, (COLUMN, COLUMN), 0)
    from_row = lax.broadcasted_iota(jnp.int32, (COLUMN, COLUMN), 1)
    before = jnp.where(((to_row >> 4) == (from_row >> 4)) & (from_row < to_row), 1.0, 0.0)
    rank = dot(before.astype(BF), member.astype(BF))
    chosen = rank == (lane & 1).astype(F32)
    weight = jnp.where(chosen, weight, 0.0)
    high = weight.astype(BF)
    w_hi[...] = high
    w_lo[...] = (weight - high.astype(F32)).astype(BF)
    sel_t[...] = jnp.where(chosen, member, 0.0).T.astype(BF)

    def select(c):
        width = CHUNKS_IN[c]
        arrived(zbuf[c].at[pl.ds(1, NZ - 1)], ("z", c))
        slots = dot(sel_t[...], zbuf[c][...].reshape(COLUMN, width)).astype(BF)
        slots = slots.reshape(4, 4, ROWS, width)
        recv1[c][0] = slots[0]
        send[c][...] = slots[1:]
        for step in range(1, 4):
            push(send[c].at[step - 1], recv1[c].at[step], ("a", c), along_a(step))

    def turn(c):
        arrived(recv1[c].at[pl.ds(1, 3)], ("a", c))
        for step in range(1, 4):
            push(recv1[c].at[:, step], recv2[c].at[step - 1], ("b", c, step), along_b(step))
        push(recv1[c].at[:, 0], sib[c].at[:, 0], ("s", c), sibling)

    def accumulate(block, half, c, first):
        rows = pl.ds(in_at[c], CHUNKS_IN[c])
        gate = dot(block, wg_v[half, rows, :])
        up = dot(block, wu_v[half, rows, :])
        if first:
            acc_g[...] = gate
            acc_u[...] = up
        else:
            acc_g[...] += gate
            acc_u[...] += up

    def landed(c):
        for step in range(1, 4):
            arrived(recv2[c].at[step - 1], ("b", c, step))
            push(recv2[c].at[step - 1], sib[c].at[:, step], ("s", c), sibling)
        if c == 0:
            loads["wg", 0].wait()
            loads["wu", 0].wait()
        width = CHUNKS_IN[c]
        block = jnp.concatenate(
            [recv1[c][:, 0].reshape(4 * ROWS, width), recv2[c][...].reshape(12 * ROWS, width)], 0
        )
        accumulate(block, 0, c, c == 0)

    def siblings(c):
        arrived(sib[c], ("s", c))
        if c == 0:
            loads["wg", 1].wait()
            loads["wu", 1].wait()
        accumulate(sib[c][...].reshape(SLOTS, CHUNKS_IN[c]), 1, c, False)

    for tick in range(n_in + 3):
        for stage, lag in ((select, 0), (turn, 1), (landed, 2), (siblings, 3)):
            if 0 <= tick - lag < n_in:
                stage(tick - lag)

    gate = acc_g[...]
    hid[...] = (gate / (1.0 + jnp.exp(-gate)) * acc_u[...]).astype(BF).reshape(4, 4, ROWS, HID)
    for step in range(4):
        push(hid.at[step], hid_sib.at[:, step], "hid", sibling)
    loads["wd"].wait()
    arrived(wd_sib, "wd")

    def down(c):
        width = CHUNKS_OUT[c]
        columns = pl.ds(out_at[c], width)
        total = dot(hid[...].reshape(SLOTS, HID), wd_own[:, columns])
        if c == 0:
            arrived(hid_sib, "hid")
        total = total + dot(hid_sib[...].reshape(SLOTS, HID), wd_sib[:, columns])
        blocks = total.astype(BF).reshape(4, 4, ROWS, width)
        ret1[c][0] = blocks[0]
        outb[c][...] = blocks[1:]
        for step in range(1, 4):
            push(outb[c].at[step - 1], ret1[c].at[step], ("rb", c), along_b(-step))

    def turn_back(c):
        arrived(ret1[c].at[pl.ds(1, 3)], ("rb", c))
        for step in range(1, 4):
            push(ret1[c].at[:, step], ret2[c].at[step - 1], ("ra", c), along_a(-step))

    def combine(c):
        width = CHUNKS_OUT[c]
        arrived(ret2[c], ("ra", c))
        block = jnp.concatenate(
            [ret1[c][:, 0].reshape(4 * ROWS, width), ret2[c][...].reshape(12 * ROWS, width)], 0
        )
        part = dot(w_hi[...], block) + dot(w_lo[...], block)
        own[c][...] = part[0:ROWS]
        zsend[c][...] = part[ROWS:].astype(BF).reshape(NZ - 1, ROWS, width)
        for step in range(1, NZ):
            push(zsend[c].at[step - 1], zrecv[c].at[step - 1], ("rz", c), along_z(-step))

    def finish(c):
        arrived(zrecv[c], ("rz", c))
        total = own[c][...] + jnp.sum(zrecv[c][...].astype(F32), 0)
        out[:, pl.ds(out_at[c], CHUNKS_OUT[c])] = total.astype(BF)

    for tick in range(n_out + 3):
        for stage, lag in ((down, 0), (turn_back, 1), (combine, 2), (finish, 3)):
            if 0 <= tick - lag < n_out:
                stage(tick - lag)

    for ref, key in sent:
        whole(ref, key).wait_send()
    assert len(index) <= send_sem.shape[0]


def layer(tokens, expert_ids, gate_scores, w_gate, w_up, w_down):
    vmem = pltpu.VMEM
    ins = lambda *lead: [vmem((*lead, ROWS, w), BF) for w in CHUNKS_IN]
    outs = lambda *lead: [vmem((*lead, ROWS, w), BF) for w in CHUNKS_OUT]
    sems = 1 + 1 + 1 + 6 * len(CHUNKS_IN) + 3 * len(CHUNKS_OUT)
    scratch = (
        ins(NZ) + ins(3, 4) + ins(4, 4) + ins(3, 4) + ins(4, 4)
        + outs(3, 4) + outs(4, 4) + outs(3, 4) + outs(NZ - 1) + outs(NZ - 1)
        + [vmem((ROWS, w), F32) for w in CHUNKS_OUT]
        + [
            vmem((TOP, ROWS), jnp.int32),
            vmem((TOP, ROWS), F32),
            vmem((NZ, 2 * ROWS, 128), F32),
            vmem((SLOTS, COLUMN), BF),
            vmem((COLUMN, SLOTS), BF),
            vmem((COLUMN, SLOTS), BF),
            vmem((4, 4, ROWS, HID), BF),
            vmem((4, 4, ROWS, HID), BF),
            vmem((SLOTS, HID), F32),
            vmem((SLOTS, HID), F32),
            vmem((2, HALF, HID), BF),
            vmem((2, HALF, HID), BF),
            vmem((HID, HALF), BF),
            vmem((HID, HALF), BF),
            pltpu.SemaphoreType.DMA((7 + len(CHUNKS_IN),)),
            pltpu.SemaphoreType.DMA((sems,)),
            pltpu.SemaphoreType.DMA((sems,)),
        ]
    )
    return pl.pallas_call(
        kernel,
        out_shape=jax.ShapeDtypeStruct((ROWS, HALF), BF),
        in_specs=[pl.BlockSpec(memory_space=pl.ANY)] * 6,
        out_specs=pl.BlockSpec(memory_space=pltpu.VMEM),
        scratch_shapes=scratch,
        compiler_params=pltpu.CompilerParams(
            collective_id=0, has_side_effects=True, vmem_limit_bytes=56 << 20
        ),
    )(tokens, expert_ids.T, gate_scores.T, w_gate, w_up, w_down)


def solution(mesh):
    in_specs = (
        P("expert", None),
        P("expert", None),
        P("expert", None),
        P("expert", None, "rep"),
        P("expert", None, "rep"),
        P("expert", "rep", None),
    )
    return jax.shard_map(layer, mesh=mesh, in_specs=in_specs, out_specs=P("expert", "rep"), check_vma=False)
```

time: 160 us -> 67.2 us (0.42)
  Pallas kernels: 0 us -> 65.4 us
  blocking collectives: 61.7 us -> 0 us
  waiting for transfers between devices: 39.7 us -> 0 us
  local copies, waits for them, and re-layouts: 18.4 us -> 1.45 us
  starting transfers between devices: 13.7 us -> 0 us
  between operations: 13.5 us -> 0.01 us
  matrix products: 9.38 us -> 0 us
  other arithmetic: 3.79 us -> 0 us
    pallas_call x0 -> x1, Pallas kernels: none -> 65.4 us  [layer(): pl.pallas_call(kernel, out_shape=jax.ShapeDtypeStruct((ROWS, HALF), BF),...]
    all_to_all x1 -> x0, blocking collectives: 61.7 us -> none  [shards(): lax.all_to_all(send_rows.reshape(devices, capacity, model_width), 'expert...]
    all_to_all x1 -> x0, waiting for transfers between devices: 27.8 us -> none  [shards(): lax.all_to_all(expert_out, 'expert', split_axis=0, concat_axis=0, tiled=T...]
    all_to_all x1 -> x0, starting transfers between devices: 13.7 us -> none  [shards(): lax.all_to_all(expert_out, 'expert', split_axis=0, concat_axis=0, tiled=T...]
    reduce_scatter x1 -> x0, waiting for transfers between devices: 11.8 us -> none  [shards(): lax.psum_scatter(partial_value, 'rep', scatter_dimension=2, tiled=True)]
    dot_general x3 -> x0, matrix products: 9.38 us -> none  [the longest x1 4.96 us: expert_rows(): return jnp.dot(hidden, down_weight, preferred_element_type=jnp.float32)]
    reshape x3 -> x0, local copies, waits for them, and re-layouts: 8.28 us -> none  [the longest x1 4.06 us: shards(): arrived.reshape(-1, model_width)]
    scatter x1 -> x0, local copies, waits for them, and re-layouts: 6.05 us -> none  [shards(): send_rows = jnp.zeros((devices * capacity, model_width), jnp.bfloat16).at...]
  transfers between devices with their start and end apart: 2 -> 0, of which waited for: 2 -> 0; matrix products, arithmetic and copies ran while one was open for 0% -> 0% of each run, Pallas kernels for 0% -> 0%
where the time goes in v1:
time: 67.2 us; the launch traced here: 66.8 us
  Pallas kernels  65.4 us (97%)
  local copies, waits for them, and re-layouts  1.45 us (2%)
    pallas_call x1, Pallas kernels, layer(): pl.pallas_call(kernel, out_shape=jax.ShapeDtypeStruct((ROWS, HALF), BF),...  65.4 us
    unnamed x1, local copies, waits for them, and re-layouts  1.45 us

profile of v1, /device:TPU:32, one launch (start us, length us, event | category | flops | bytes accessed | tf_op | source)
XLA Modules:
  0.0 66.8 jit_solution(8432238672410170506)
XLA Ops:
  0.0 65.4 %shard_map.64 = bf16[16,1792]{1,0:T(8,128)(2,1)} custom-call(bf16[16,3584]{1,0:T(8,128)(2,1)} %tok.1, s32[8,16]{1,0:T(8,128)} %bitcast.2, f32[8,16]{1,0:T(8,128)} %bitcast.3, bf16[1,3584,512]{2,1,0:T(8,128)(2,1)} %wg.1, bf16[1,3584,512]{2,1,0:T(8,128)(2,1)} %wu.1, bf16[1,512,3584]{2,1,0:T(8,128)(2,1)} %wd.1), custom_call_target="tpu_custom_call" | custom-call | tf_op jit(solution)/shard_map/pallas_call | solution.py:298
  65.4 1.4 %copy.8 = bf16[16,1792]{1,0:T(8,128)(2,1)} copy(bf16[16,1792]{1,0:T(8,128)(2,1)} %shard_map.64) | data formatting | bytes 114688

commit v2 on v1

v2 whole, which is shorter than its diff:
```python
import jax
import jax.numpy as jnp
from jax import lax
from jax.experimental import pallas as pl
from jax.experimental.pallas import tpu as pltpu
from jax.sharding import PartitionSpec as P

NX, NY, NZ = 4, 4, 8
ROWS = 16
TOP = 8
CAP = 2
HALF = 1792
HID = 512
SLOTS = NX * NY * NZ * CAP
COLUMN = NZ * ROWS
PLANE = NX * NY
Z_ORDER = (4, 3, 5, 2, 6, 1, 7)
PLANE_ORDER = (10, 9, 11, 6, 14, 5, 7, 13, 15, 8, 2, 4, 12, 1, 3)
LAG = 2
CHUNKS_IN = (256, 512, 512, 512)
CHUNKS_OUT = (512, 512, 512, 256)
BF = jnp.bfloat16
F32 = jnp.float32


def starts(widths):
    return [sum(widths[:i]) for i in range(len(widths))]


def dot(lhs, rhs):
    return jnp.dot(lhs, rhs, preferred_element_type=F32)


def kernel(tok, ids, sc, wg, wu, wd, out, *scratch):
    names = iter(scratch)
    n_in, n_out = len(CHUNKS_IN), len(CHUNKS_OUT)
    take = lambda n: [next(names) for _ in range(n)]
    zbuf, send, recv, sib = (take(n_in) for _ in range(4))
    outb, ret, zsend, zrecv, own = (take(n_out) for _ in range(5))
    ids_v, sc_v, meta, sel_t, w_hi, w_lo, hid, hid_sib, acc_g, acc_u = take(10)
    wg_v, wu_v, wd_own, wd_sib = take(4)
    local, send_sem, recv_sem = take(3)

    r = lax.axis_index("rep")
    e = lax.axis_index("expert")
    y, z, x = e // 32, (e // 4) % 8, e % 4

    def in_plane(block, sign):
        y_at = (y + sign * (block // 4) + 4) % 4
        x_at = (x + sign * (block % 4) + 4) % 4
        return {"rep": r, "expert": (y_at * 8 + z) * 4 + x_at}

    def along_z(step):
        return {"rep": r, "expert": (y * 8 + (z + step + 8) % 8) * 4 + x}

    sibling = {"rep": 1 - r, "expert": e}

    index = {}

    def sem_of(key):
        return index.setdefault(key, len(index))

    def push(src, dst, key, target):
        at = sem_of(key)
        pltpu.make_async_remote_copy(
            src_ref=src,
            dst_ref=dst,
            send_sem=send_sem.at[at],
            recv_sem=recv_sem.at[at],
            device_id=target,
        ).start()

    def whole(ref, key):
        at = sem_of(key)
        return pltpu.make_async_remote_copy(
            src_ref=ref,
            dst_ref=ref,
            send_sem=send_sem.at[at],
            recv_sem=recv_sem.at[at],
            device_id=sibling,
        )

    sent = []

    def arrived(ref, key):
        whole(ref, key).wait_recv()
        sent.append((ref, key))

    in_at, out_at = starts(CHUNKS_IN), starts(CHUNKS_OUT)
    mine, other = r * HALF, (1 - r) * HALF

    loads = {}

    def load(name, src, dst):
        loads[name] = pltpu.make_async_copy(src, dst, local.at[len(loads)])
        loads[name].start()

    load("ids", ids, ids_v)
    load("sc", sc, sc_v)
    for c, width in enumerate(CHUNKS_IN):
        load(("tok", c), tok.at[:, pl.ds(pl.multiple_of(mine + in_at[c], 128), width)], zbuf[c].at[0])

    barrier = pltpu.get_barrier_semaphore()
    for step in range(1, NZ):
        pl.semaphore_signal(barrier, inc=1, device_id=along_z(step))
    for block in range(1, PLANE):
        pl.semaphore_signal(barrier, inc=1, device_id=in_plane(block, 1))
    pl.semaphore_signal(barrier, inc=1, device_id=sibling)

    for half, base in ((0, mine), (1, other)):
        rows = pl.ds(pl.multiple_of(base, 128), HALF)
        load(("wg", half), wg.at[0, rows, :], wg_v.at[half])
        load(("wu", half), wu.at[0, rows, :], wu_v.at[half])
    load("wd", wd.at[0, :, pl.ds(pl.multiple_of(mine, 128), HALF)], wd_own)
    loads["ids"].wait()
    loads["sc"].wait()
    meta[0, :, 0 : 2 * ROWS] = jnp.concatenate([ids_v[...].astype(F32), sc_v[...]], 1)
    for c in range(n_in):
        loads["tok", c].wait()
    pl.semaphore_wait(barrier, NZ - 1 + PLANE - 1 + 1)

    for step in Z_ORDER:
        push(meta.at[0], meta.at[step], "meta", along_z(step))
    for c in range(n_in):
        for step in Z_ORDER:
            push(zbuf[c].at[0], zbuf[c].at[step], ("z", c), along_z(step))
    push(wd.at[0, :, pl.ds(pl.multiple_of(other, 128), HALF)], wd_sib, "wd", sibling)

    lane = lax.broadcasted_iota(jnp.int32, (ROWS, SLOTS), 1)
    y_to = (y + (lane >> 6)) & 3
    x_to = (x + ((lane >> 4) & 3)) & 3
    named = ((y_to * 8 + z) * 4 + x_to).astype(F32)
    to_row = lax.broadcasted_iota(jnp.int32, (COLUMN, COLUMN), 0)
    from_row = lax.broadcasted_iota(jnp.int32, (COLUMN, COLUMN), 1)
    before = jnp.where(((to_row >> 4) == (from_row >> 4)) & (from_row < to_row), 1.0, 0.0).astype(BF)
    lane_all = lax.broadcasted_iota(jnp.int32, (COLUMN, SLOTS), 1)
    arrived(meta.at[pl.ds(1, NZ - 1)], "meta")
    table = meta[...].reshape(NZ * TOP, 128).T
    members, weights = [], []
    for step in range(NZ):
        expert = jnp.where(((lane >> 1) & 7) == step, named, -1.0)
        member = jnp.zeros((ROWS, SLOTS), F32)
        weight = jnp.zeros((ROWS, SLOTS), F32)
        for k in range(TOP):
            at = step * TOP + k
            hit = table[0:ROWS, at : at + 1] == expert
            member = jnp.where(hit, 1.0, member)
            weight = jnp.where(hit, table[ROWS : 2 * ROWS, at : at + 1], weight)
        members.append(member)
        weights.append(weight)
    member = jnp.concatenate(members, 0)
    weight = jnp.concatenate(weights, 0)
    chosen = dot(before, member.astype(BF)) == (lane_all & 1).astype(F32)
    sel_t[...] = jnp.where(chosen, member, 0.0).T.astype(BF)
    weight = jnp.where(chosen, weight, 0.0)
    high = weight.astype(BF)
    w_hi[...] = high
    w_lo[...] = (weight - high.astype(F32)).astype(BF)

    def select(c):
        width = CHUNKS_IN[c]
        arrived(zbuf[c].at[pl.ds(1, NZ - 1)], ("z", c))
        slots = dot(sel_t[...], zbuf[c][...].reshape(COLUMN, width)).astype(BF)
        slots = slots.reshape(PLANE, ROWS, width)
        recv[c][0] = slots[0]
        send[c][...] = slots[1:]
        for block in PLANE_ORDER:
            push(send[c].at[block - 1], recv[c].at[block], ("p", c), in_plane(block, 1))

    def accumulate(block, half, c, first):
        rows = pl.ds(in_at[c], CHUNKS_IN[c])
        gate = dot(block, wg_v[half, rows, :])
        up = dot(block, wu_v[half, rows, :])
        if first:
            acc_g[...] = gate
            acc_u[...] = up
        else:
            acc_g[...] += gate
            acc_u[...] += up

    def landed(c):
        arrived(recv[c].at[pl.ds(1, PLANE - 1)], ("p", c))
        push(recv[c], sib[c], ("s", c), sibling)
        if c == 0:
            loads["wg", 0].wait()
            loads["wu", 0].wait()
        accumulate(recv[c][...].reshape(SLOTS, CHUNKS_IN[c]), 0, c, c == 0)

    def siblings(c):
        arrived(sib[c], ("s", c))
        if c == 0:
            loads["wg", 1].wait()
            loads["wu", 1].wait()
        accumulate(sib[c][...].reshape(SLOTS, CHUNKS_IN[c]), 1, c, False)

    for tick in range(n_in + 2):
        for stage, lag in ((select, 0), (landed, 1), (siblings, 2)):
            if 0 <= tick - lag < n_in:
                stage(tick - lag)

    gate = acc_g[...]
    hid[...] = (gate / (1.0 + jnp.exp(-gate)) * acc_u[...]).astype(BF)
    push(hid, hid_sib, "hid", sibling)
    loads["wd"].wait()
    arrived(wd_sib, "wd")

    def down(c):
        width = CHUNKS_OUT[c]
        columns = pl.ds(out_at[c], width)
        total = dot(hid[...], wd_own[:, columns])
        if c == 0:
            arrived(hid_sib, "hid")
        total = total + dot(hid_sib[...], wd_sib[:, columns])
        blocks = total.astype(BF).reshape(PLANE, ROWS, width)
        ret[c][0] = blocks[0]
        outb[c][...] = blocks[1:]
        for block in PLANE_ORDER:
            push(outb[c].at[block - 1], ret[c].at[block], ("rp", c), in_plane(block, -1))

    def combine(c):
        width = CHUNKS_OUT[c]
        arrived(ret[c].at[pl.ds(1, PLANE - 1)], ("rp", c))
        block = ret[c][...].reshape(SLOTS, width)
        part = dot(w_hi[...], block) + dot(w_lo[...], block)
        own[c][...] = part[0:ROWS]
        zsend[c][...] = part[ROWS:].astype(BF).reshape(NZ - 1, ROWS, width)
        for step in Z_ORDER:
            push(zsend[c].at[step - 1], zrecv[c].at[step - 1], ("rz", c), along_z(-step))

    def finish(c):
        arrived(zrecv[c], ("rz", c))
        total = own[c][...] + jnp.sum(zrecv[c][...].astype(F32), 0)
        out[:, pl.ds(out_at[c], CHUNKS_OUT[c])] = total.astype(BF)

    for tick in range(n_out + LAG + 1):
        for stage, lag in ((down, 0), (combine, LAG), (finish, LAG + 1)):
            if 0 <= tick - lag < n_out:
                stage(tick - lag)

    for ref, key in sent:
        whole(ref, key).wait_send()
    assert len(index) <= send_sem.shape[0]


def layer(tokens, expert_ids, gate_scores, w_gate, w_up, w_down):
    vmem = pltpu.VMEM
    ins = lambda *lead: [vmem((*lead, ROWS, w), BF) for w in CHUNKS_IN]
    outs = lambda *lead: [vmem((*lead, ROWS, w), BF) for w in CHUNKS_OUT]
    sems = 3 + 3 * len(CHUNKS_IN) + 2 * len(CHUNKS_OUT)
    scratch = (
        ins(NZ) + ins(PLANE - 1) + ins(PLANE) + ins(PLANE)
        + outs(PLANE - 1) + outs(PLANE) + outs(NZ - 1) + outs(NZ - 1)
        + [vmem((ROWS, w), F32) for w in CHUNKS_OUT]
        + [
            vmem((TOP, ROWS), jnp.int32),
            vmem((TOP, ROWS), F32),
            vmem((NZ, TOP, 128), F32),
            vmem((SLOTS, COLUMN), BF),
            vmem((COLUMN, SLOTS), BF),
            vmem((COLUMN, SLOTS), BF),
            vmem((SLOTS, HID), BF),
            vmem((SLOTS, HID), BF),
            vmem((SLOTS, HID), F32),
            vmem((SLOTS, HID), F32),
            vmem((2, HALF, HID), BF),
            vmem((2, HALF, HID), BF),
            vmem((HID, HALF), BF),
            vmem((HID, HALF), BF),
            pltpu.SemaphoreType.DMA((7 + len(CHUNKS_IN),)),
            pltpu.SemaphoreType.DMA((sems,)),
            pltpu.SemaphoreType.DMA((sems,)),
        ]
    )
    return pl.pallas_call(
        kernel,
        out_shape=jax.ShapeDtypeStruct((ROWS, HALF), BF),
        in_specs=[pl.BlockSpec(memory_space=pl.ANY)] * 6,
        out_specs=pl.BlockSpec(memory_space=pltpu.VMEM),
        scratch_shapes=scratch,
        compiler_params=pltpu.CompilerParams(
            collective_id=0, has_side_effects=True, vmem_limit_bytes=56 << 20
        ),
    )(tokens, expert_ids.T, gate_scores.T, w_gate, w_up, w_down)


def solution(mesh):
    in_specs = (
        P("expert", None),
        P("expert", None),
        P("expert", None),
        P("expert", None, "rep"),
        P("expert", None, "rep"),
        P("expert", "rep", None),
    )
    return jax.shard_map(layer, mesh=mesh, in_specs=in_specs, out_specs=P("expert", "rep"), check_vma=False)
```

time: 67.2 us -> 56.2 us (0.84)
  Pallas kernels: 65.4 us -> 54.1 us
    pallas_call x1, Pallas kernels: 65.4 us -> 54.1 us  [layer(): pl.pallas_call(kernel, out_shape=jax.ShapeDtypeStruct((ROWS, HALF), BF),...]
where the time goes in v2:
time: 56.2 us; the launch traced here: 55.6 us
  Pallas kernels  54.1 us (96%)
  local copies, waits for them, and re-layouts  1.45 us (3%)
    pallas_call x1, Pallas kernels, layer(): pl.pallas_call(kernel, out_shape=jax.ShapeDtypeStruct((ROWS, HALF), BF),...  54.1 us
    unnamed x1, local copies, waits for them, and re-layouts  1.45 us

profile of v2, /device:TPU:32, one launch (start us, length us, event | category | flops | bytes accessed | tf_op | source)
XLA Modules:
  0.0 55.6 jit_solution(12612932773285775047)
XLA Ops:
  0.0 54.1 %shard_map.64 = bf16[16,1792]{1,0:T(8,128)(2,1)} custom-call(bf16[16,3584]{1,0:T(8,128)(2,1)} %tok.1, s32[8,16]{1,0:T(8,128)} %bitcast.2, f32[8,16]{1,0:T(8,128)} %bitcast.3, bf16[1,3584,512]{2,1,0:T(8,128)(2,1)} %wg.1, bf16[1,3584,512]{2,1,0:T(8,128)(2,1)} %wu.1, bf16[1,512,3584]{2,1,0:T(8,128)(2,1)} %wd.1), custom_call_target="tpu_custom_call" | custom-call | tf_op jit(solution)/shard_map/pallas_call | solution.py:274
  54.1 1.4 %copy.8 = bf16[16,1792]{1,0:T(8,128)(2,1)} copy(bf16[16,1792]{1,0:T(8,128)(2,1)} %shard_map.64) | data formatting | bytes 114688

commit v3 on v2

--- a/solution.py
+++ b/solution.py
@@ -16,8 +16,9 @@
 PLANE = NX * NY
 Z_ORDER = (4, 3, 5, 2, 6, 1, 7)
 PLANE_ORDER = (10, 9, 11, 6, 14, 5, 7, 13, 15, 8, 2, 4, 12, 1, 3)
-LAG = 2
-CHUNKS_IN = (256, 512, 512, 512)
+IN_STEPS = "S0S1S2F0M0S3F1M1X0F2M2X1F3M3X2X3"
+OUT_STEPS = "D0D1D2C0D3C1C2N0C3N1N2N3"
+CHUNKS_IN = (512, 512, 512, 256)
 CHUNKS_OUT = (512, 512, 512, 256)
 BF = jnp.bfloat16
 F32 = jnp.float32
@@ -107,14 +108,10 @@
         pl.semaphore_signal(barrier, inc=1, device_id=in_plane(block, 1))
     pl.semaphore_signal(barrier, inc=1, device_id=sibling)
 
-    for half, base in ((0, mine), (1, other)):
-        rows = pl.ds(pl.multiple_of(base, 128), HALF)
-        load(("wg", half), wg.at[0, rows, :], wg_v.at[half])
-        load(("wu", half), wu.at[0, rows, :], wu_v.at[half])
-    load("wd", wd.at[0, :, pl.ds(pl.multiple_of(mine, 128), HALF)], wd_own)
     loads["ids"].wait()
     loads["sc"].wait()
-    meta[0, :, 0 : 2 * ROWS] = jnp.concatenate([ids_v[...].astype(F32), sc_v[...]], 1)
+    high = sc_v[...].astype(BF).astype(F32)
+    meta[0, :, 0 : 3 * ROWS] = jnp.concatenate([ids_v[...].astype(F32), high, sc_v[...] - high], 1).astype(BF)
     for c in range(n_in):
         loads["tok", c].wait()
     pl.semaphore_wait(barrier, NZ - 1 + PLANE - 1 + 1)
@@ -124,7 +121,6 @@
     for c in range(n_in):
         for step in Z_ORDER:
             push(zbuf[c].at[0], zbuf[c].at[step], ("z", c), along_z(step))
-    push(wd.at[0, :, pl.ds(pl.multiple_of(other, 128), HALF)], wd_sib, "wd", sibling)
 
     lane = lax.broadcasted_iota(jnp.int32, (ROWS, SLOTS), 1)
     y_to = (y + (lane >> 6)) & 3
@@ -135,27 +131,33 @@
     before = jnp.where(((to_row >> 4) == (from_row >> 4)) & (from_row < to_row), 1.0, 0.0).astype(BF)
     lane_all = lax.broadcasted_iota(jnp.int32, (COLUMN, SLOTS), 1)
     arrived(meta.at[pl.ds(1, NZ - 1)], "meta")
-    table = meta[...].reshape(NZ * TOP, 128).T
-    members, weights = [], []
+    for half, base in ((0, mine), (1, other)):
+        rows = pl.ds(pl.multiple_of(base, 128), HALF)
+        load(("wg", half), wg.at[0, rows, :], wg_v.at[half])
+        load(("wu", half), wu.at[0, rows, :], wu_v.at[half])
+    load("wd", wd.at[0, :, pl.ds(pl.multiple_of(mine, 128), HALF)], wd_own)
+    push(wd.at[0, :, pl.ds(pl.multiple_of(other, 128), HALF)], wd_sib, "wd", sibling)
+    table = meta[...].reshape(NZ * TOP, 128).astype(F32).T
+    members, highs, lows = [], [], []
     for step in range(NZ):
         expert = jnp.where(((lane >> 1) & 7) == step, named, -1.0)
         member = jnp.zeros((ROWS, SLOTS), F32)
-        weight = jnp.zeros((ROWS, SLOTS), F32)
+        high = jnp.zeros((ROWS, SLOTS), F32)
+        low = jnp.zeros((ROWS, SLOTS), F32)
         for k in range(TOP):
             at = step * TOP + k
             hit = table[0:ROWS, at : at + 1] == expert
             member = jnp.where(hit, 1.0, member)
-            weight = jnp.where(hit, table[ROWS : 2 * ROWS, at : at + 1], weight)
+            high = jnp.where(hit, table[ROWS : 2 * ROWS, at : at + 1], high)
+            low = jnp.where(hit, table[2 * ROWS : 3 * ROWS, at : at + 1], low)
         members.append(member)
-        weights.append(weight)
+        highs.append(high)
+        lows.append(low)
     member = jnp.concatenate(members, 0)
-    weight = jnp.concatenate(weights, 0)
     chosen = dot(before, member.astype(BF)) == (lane_all & 1).astype(F32)
     sel_t[...] = jnp.where(chosen, member, 0.0).T.astype(BF)
-    weight = jnp.where(chosen, weight, 0.0)
-    high = weight.astype(BF)
-    w_hi[...] = high
-    w_lo[...] = (weight - high.astype(F32)).astype(BF)
+    w_hi[...] = jnp.where(chosen, jnp.concatenate(highs, 0), 0.0).astype(BF)
+    w_lo[...] = jnp.where(chosen, jnp.concatenate(lows, 0), 0.0).astype(BF)
 
     def select(c):
         width = CHUNKS_IN[c]
@@ -181,6 +183,8 @@
     def landed(c):
         arrived(recv[c].at[pl.ds(1, PLANE - 1)], ("p", c))
         push(recv[c], sib[c], ("s", c), sibling)
+
+    def halves(c):
         if c == 0:
             loads["wg", 0].wait()
             loads["wu", 0].wait()
@@ -193,10 +197,9 @@
             loads["wu", 1].wait()
         accumulate(sib[c][...].reshape(SLOTS, CHUNKS_IN[c]), 1, c, False)
 
-    for tick in range(n_in + 2):
-        for stage, lag in ((select, 0), (landed, 1), (siblings, 2)):
-            if 0 <= tick - lag < n_in:
-                stage(tick - lag)
+    stages = {"S": select, "F": landed, "M": halves, "X": siblings}
+    for name, c in zip(IN_STEPS[::2], IN_STEPS[1::2]):
+        stages[name](int(c))
 
     gate = acc_g[...]
     hid[...] = (gate / (1.0 + jnp.exp(-gate)) * acc_u[...]).astype(BF)
@@ -232,10 +235,9 @@
         total = own[c][...] + jnp.sum(zrecv[c][...].astype(F32), 0)
         out[:, pl.ds(out_at[c], CHUNKS_OUT[c])] = total.astype(BF)
 
-    for tick in range(n_out + LAG + 1):
-        for stage, lag in ((down, 0), (combine, LAG), (finish, LAG + 1)):
-            if 0 <= tick - lag < n_out:
-                stage(tick - lag)
+    stages = {"D": down, "C": combine, "N": finish}
+    for name, c in zip(OUT_STEPS[::2], OUT_STEPS[1::2]):
+        stages[name](int(c))
 
     for ref, key in sent:
         whole(ref, key).wait_send()
@@ -254,7 +256,7 @@
         + [
             vmem((TOP, ROWS), jnp.int32),
             vmem((TOP, ROWS), F32),
-            vmem((NZ, TOP, 128), F32),
+            vmem((NZ, TOP, 128), BF),
             vmem((SLOTS, COLUMN), BF),
             vmem((COLUMN, SLOTS), BF),
             vmem((COLUMN, SLOTS), BF),

time: 56.2 us -> 53.1 us (0.945)
  Pallas kernels: 54.1 us -> 51.1 us
    pallas_call x1, Pallas kernels: 54.1 us -> 51.1 us  [layer(): pl.pallas_call(kernel, out_shape=jax.ShapeDtypeStruct((ROWS, HALF), BF),...]
where the time goes in v3:
time: 53.1 us; the launch traced here: 52.6 us
  Pallas kernels  51.1 us (96%)
  local copies, waits for them, and re-layouts  1.45 us (3%)
    pallas_call x1, Pallas kernels, layer(): pl.pallas_call(kernel, out_shape=jax.ShapeDtypeStruct((ROWS, HALF), BF),...  51.1 us
    unnamed x1, local copies, waits for them, and re-layouts  1.45 us

profile of v3, /device:TPU:32, one launch (start us, length us, event | category | flops | bytes accessed | tf_op | source)
XLA Modules:
  0.0 52.6 jit_solution(6420025346082718268)
XLA Ops:
  0.0 51.1 %shard_map.64 = bf16[16,1792]{1,0:T(8,128)(2,1)} custom-call(bf16[16,3584]{1,0:T(8,128)(2,1)} %tok.1, s32[8,16]{1,0:T(8,128)} %bitcast.2, f32[8,16]{1,0:T(8,128)} %bitcast.3, bf16[1,3584,512]{2,1,0:T(8,128)(2,1)} %wg.1, bf16[1,3584,512]{2,1,0:T(8,128)(2,1)} %wu.1, bf16[1,512,3584]{2,1,0:T(8,128)(2,1)} %wd.1), custom_call_target="tpu_custom_call" | custom-call | tf_op jit(solution)/shard_map/pallas_call | solution.py:276
  51.1 1.4 %copy.8 = bf16[16,1792]{1,0:T(8,128)(2,1)} copy(bf16[16,1792]{1,0:T(8,128)(2,1)} %shard_map.64) | data formatting | bytes 114688

commit v4 on v3

v4 whole, which is shorter than its diff:
```python
import jax
import jax.numpy as jnp
from jax import lax
from jax.experimental import pallas as pl
from jax.experimental.pallas import tpu as pltpu
from jax.sharding import PartitionSpec as P

NX, NY, NZ = 4, 4, 8
ROWS = 16
TOP = 8
CAP = 2
HALF = 1792
HID = 512
SLOTS = NX * NY * NZ * CAP
PLANE = NX * NY
Z_ORDER = (4, 2, 6, 3, 5, 1, 7)
PLANE_ORDER = (10, 9, 11, 6, 14, 5, 7, 13, 15, 8, 2, 4, 12, 1, 3)
STEPS = "S00 S01 S10 F00 M00 S11 F01 M01 X00 X01 H00 F10 M10 D00 D01 F11 M11 X10 X11 H10 D10 D11 C00 C01 C10 C11 N00 N01 N10 N11"
CHUNKS_IN = ((768, 1024), (1024, 768))
CHUNKS_OUT = ((1024, 768), (1024, 768))
GROUPS = ((0, 2, 4, 6), (1, 3, 5, 7))
Z_ORDERS = ((2, 1, 3), (1, 2, 0, 3))
PER = len(GROUPS[0])
GROUP_ROWS = PER * ROWS
BLOCK = PER * CAP
GROUP_SLOTS = SLOTS // 2
BF = jnp.bfloat16
F32 = jnp.float32


def starts(widths):
    return [sum(widths[:i]) for i in range(len(widths))]


def dot(lhs, rhs):
    return jnp.dot(lhs, rhs, preferred_element_type=F32)


def kernel(tok, ids, sc, wg, wu, wd, out, *scratch):
    names = iter(scratch)
    take = lambda n: [next(names) for _ in range(n)]
    per_group = lambda lists: [take(len(widths)) for widths in lists]
    zbuf, send, recv, sib = (per_group(CHUNKS_IN) for _ in range(4))
    outb, ret, zsend, zrecv = (per_group(CHUNKS_OUT) for _ in range(4))
    ids_v, sc_v, meta, sel_t, w_hi, w_lo, hid, hid_sib, acc_g, acc_u, own = take(11)
    wg_v, wu_v, wd_own, wd_sib, tok_v = take(5)
    local, send_sem, recv_sem = take(3)

    r = lax.axis_index("rep")
    e = lax.axis_index("expert")
    y, z, x = e // 32, (e // 4) % 8, e % 4

    def in_plane(block, sign):
        y_at = (y + sign * (block // 4) + 4) % 4
        x_at = (x + sign * (block % 4) + 4) % 4
        return {"rep": r, "expert": (y_at * 8 + z) * 4 + x_at}

    def along_z(step):
        return {"rep": r, "expert": (y * 8 + (z + step + 8) % 8) * 4 + x}

    sibling = {"rep": 1 - r, "expert": e}

    index = {}

    def sem_of(key):
        return index.setdefault(key, len(index))

    def push(src, dst, key, target):
        at = sem_of(key)
        pltpu.make_async_remote_copy(
            src_ref=src,
            dst_ref=dst,
            send_sem=send_sem.at[at],
            recv_sem=recv_sem.at[at],
            device_id=target,
        ).start()

    def whole(ref, key):
        at = sem_of(key)
        return pltpu.make_async_remote_copy(
            src_ref=ref,
            dst_ref=ref,
            send_sem=send_sem.at[at],
            recv_sem=recv_sem.at[at],
            device_id=sibling,
        )

    sent = []

    def arrived(ref, key):
        whole(ref, key).wait_recv()
        sent.append((ref, key))

    in_at, out_at = [starts(w) for w in CHUNKS_IN], [starts(w) for w in CHUNKS_OUT]
    mine, other = r * HALF, (1 - r) * HALF

    loads = {}

    def load(name, src, dst):
        loads[name] = pltpu.make_async_copy(src, dst, local.at[len(loads)])
        loads[name].start()

    load("ids", ids, ids_v)
    load("sc", sc, sc_v)
    load("tok", tok.at[:, pl.ds(pl.multiple_of(mine, 128), HALF)], tok_v)

    barrier = pltpu.get_barrier_semaphore()
    for step in range(1, NZ):
        pl.semaphore_signal(barrier, inc=1, device_id=along_z(step))
    for block in range(1, PLANE):
        pl.semaphore_signal(barrier, inc=1, device_id=in_plane(block, 1))
    pl.semaphore_signal(barrier, inc=1, device_id=sibling)

    loads["ids"].wait()
    loads["sc"].wait()
    high = sc_v[...].astype(BF).astype(F32)
    meta[0, :, 0 : 3 * ROWS] = jnp.concatenate([ids_v[...].astype(F32), high, sc_v[...] - high], 1).astype(BF)
    loads["tok"].wait()
    for c, width in enumerate(CHUNKS_IN[0]):
        zbuf[0][c][0] = tok_v[:, in_at[0][c] : in_at[0][c] + width]
    pl.semaphore_wait(barrier, NZ - 1 + PLANE - 1 + 1)

    for step in Z_ORDER:
        push(meta.at[0], meta.at[step], "meta", along_z(step))
    for g in range(2):
        for c, width in enumerate(CHUNKS_IN[g]):
            for p in Z_ORDERS[g]:
                push(
                    tok_v.at[:, pl.ds(in_at[g][c], width)],
                    zbuf[g][c].at[p],
                    ("z", g, c),
                    along_z(GROUPS[g][p]),
                )

    lane = lax.broadcasted_iota(jnp.int32, (ROWS, GROUP_SLOTS), 1)
    y_to = (y + (lane >> 5)) & 3
    x_to = (x + ((lane >> 3) & 3)) & 3
    named = ((y_to * 8 + z) * 4 + x_to).astype(F32)
    to_row = lax.broadcasted_iota(jnp.int32, (GROUP_ROWS, GROUP_ROWS), 0)
    from_row = lax.broadcasted_iota(jnp.int32, (GROUP_ROWS, GROUP_ROWS), 1)
    before = jnp.where(((to_row >> 4) == (from_row >> 4)) & (from_row < to_row), 1.0, 0.0).astype(BF)
    lane_all = lax.broadcasted_iota(jnp.int32, (GROUP_ROWS, GROUP_SLOTS), 1)
    arrived(meta.at[pl.ds(1, NZ - 1)], "meta")
    for half, base in ((0, mine), (1, other)):
        rows = pl.ds(pl.multiple_of(base, 128), HALF)
        load(("wg", half), wg.at[0, rows, :], wg_v.at[half])
        load(("wu", half), wu.at[0, rows, :], wu_v.at[half])
    load("wd", wd.at[0, :, pl.ds(pl.multiple_of(mine, 128), HALF)], wd_own)
    push(wd.at[0, :, pl.ds(pl.multiple_of(other, 128), HALF)], wd_sib, "wd", sibling)
    table = meta[...].reshape(NZ * TOP, 128).astype(F32).T
    for g in range(2):
        members, highs, lows = [], [], []
        for p, step in enumerate(GROUPS[g]):
            expert = jnp.where(((lane >> 1) & 3) == p, named, -1.0)
            member = jnp.zeros((ROWS, GROUP_SLOTS), F32)
            high = jnp.zeros((ROWS, GROUP_SLOTS), F32)
            low = jnp.zeros((ROWS, GROUP_SLOTS), F32)
            for k in range(TOP):
                at = step * TOP + k
                hit = table[0:ROWS, at : at + 1] == expert
                member = jnp.where(hit, 1.0, member)
                high = jnp.where(hit, table[ROWS : 2 * ROWS, at : at + 1], high)
                low = jnp.where(hit, table[2 * ROWS : 3 * ROWS, at : at + 1], low)
            members.append(member)
            highs.append(high)
            lows.append(low)
        member = jnp.concatenate(members, 0)
        chosen = dot(before, member.astype(BF)) == (lane_all & 1).astype(F32)
        sel_t[g] = jnp.where(chosen, member, 0.0).T.astype(BF)
        w_hi[g] = jnp.where(chosen, jnp.concatenate(highs, 0), 0.0).astype(BF)
        w_lo[g] = jnp.where(chosen, jnp.concatenate(lows, 0), 0.0).astype(BF)

    ready = set()

    def once(*keys):
        for key in keys:
            if key not in ready:
                ready.add(key)
                loads[key].wait()

    def far(g):
        return pl.ds(1 - g, PER - 1 + g)

    def select(g, c):
        width = CHUNKS_IN[g][c]
        arrived(zbuf[g][c].at[far(g)], ("z", g, c))
        slots = dot(sel_t[g], zbuf[g][c][...].reshape(GROUP_ROWS, width)).astype(BF)
        slots = slots.reshape(PLANE, BLOCK, width)
        recv[g][c][0] = slots[0]
        send[g][c][...] = slots[1:]
        for block in PLANE_ORDER:
            push(send[g][c].at[block - 1], recv[g][c].at[block], ("p", g, c), in_plane(block, 1))

    def accumulate(g, block, half, c, first):
        rows = pl.ds(in_at[g][c], CHUNKS_IN[g][c])
        gate = dot(block, wg_v[half, rows, :])
        up = dot(block, wu_v[half, rows, :])
        if first:
            acc_g[g] = gate
            acc_u[g] = up
        else:
            acc_g[g] += gate
            acc_u[g] += up

    def forward(g, c):
        arrived(recv[g][c].at[pl.ds(1, PLANE - 1)], ("p", g, c))
        push(recv[g][c], sib[g][c], ("s", g, c), sibling)

    def halves(g, c):
        once(("wg", 0), ("wu", 0))
        accumulate(g, recv[g][c][...].reshape(GROUP_SLOTS, CHUNKS_IN[g][c]), 0, c, c == 0)

    def siblings(g, c):
        arrived(sib[g][c], ("s", g, c))
        once(("wg", 1), ("wu", 1))
        accumulate(g, sib[g][c][...].reshape(GROUP_SLOTS, CHUNKS_IN[g][c]), 1, c, False)

    def hidden(g, c):
        gate = acc_g[g]
        hid[g] = (gate / (1.0 + jnp.exp(-gate)) * acc_u[g]).astype(BF)
        push(hid.at[g], hid_sib.at[g], ("hid", g), sibling)

    def down(g, c):
        width = CHUNKS_OUT[g][c]
        columns = pl.ds(out_at[g][c], width)
        once("wd")
        total = dot(hid[g], wd_own[:, columns])
        if c == 0:
            if g == 0:
                arrived(wd_sib, "wd")
            arrived(hid_sib.at[g], ("hid", g))
        total = total + dot(hid_sib[g], wd_sib[:, columns])
        blocks = total.astype(BF).reshape(PLANE, BLOCK, width)
        ret[g][c][0] = blocks[0]
        outb[g][c][...] = blocks[1:]
        for block in PLANE_ORDER:
            push(outb[g][c].at[block - 1], ret[g][c].at[block], ("rp", g, c), in_plane(block, -1))

    def combine(g, c):
        width = CHUNKS_OUT[g][c]
        arrived(ret[g][c].at[pl.ds(1, PLANE - 1)], ("rp", g, c))
        block = ret[g][c][...].reshape(GROUP_SLOTS, width)
        part = dot(w_hi[g], block) + dot(w_lo[g], block)
        if g == 0:
            own[:, pl.ds(out_at[g][c], width)] = part[0:ROWS]
        zsend[g][c][...] = part.astype(BF).reshape(PER, ROWS, width)
        for p in Z_ORDERS[g]:
            push(zsend[g][c].at[p], zrecv[g][c].at[p], ("rz", g, c), along_z(-GROUPS[g][p]))

    def finish(g, c):
        arrived(zrecv[g][c].at[far(g)], ("rz", g, c))
        columns = pl.ds(out_at[g][c], CHUNKS_OUT[g][c])
        total = own[:, columns] + jnp.sum(zrecv[g][c][far(g)].astype(F32), 0)
        if g == 0:
            own[:, columns] = total
        else:
            out[:, columns] = total.astype(BF)

    stages = {
        "S": select, "F": forward, "M": halves, "X": siblings,
        "H": hidden, "D": down, "C": combine, "N": finish,
    }
    for name, g, c in STEPS.split():
        stages[name](int(g), int(c))

    for ref, key in sent:
        whole(ref, key).wait_send()
    assert len(index) <= send_sem.shape[0]


def layer(tokens, expert_ids, gate_scores, w_gate, w_up, w_down):
    vmem = pltpu.VMEM
    ins = lambda *lead: [vmem((*lead, w), BF) for widths in CHUNKS_IN for w in widths]
    outs = lambda *lead: [vmem((*lead, w), BF) for widths in CHUNKS_OUT for w in widths]
    sems = 4 + 3 * len(sum(CHUNKS_IN, ())) + 2 * len(sum(CHUNKS_OUT, ()))
    scratch = (
        ins(PER, ROWS) + ins(PLANE - 1, BLOCK) + ins(PLANE, BLOCK) + ins(PLANE, BLOCK)
        + outs(PLANE - 1, BLOCK) + outs(PLANE, BLOCK) + outs(PER, ROWS) + outs(PER, ROWS)
        + [
            vmem((TOP, ROWS), jnp.int32),
            vmem((TOP, ROWS), F32),
            vmem((NZ, TOP, 128), BF),
            vmem((2, GROUP_SLOTS, GROUP_ROWS), BF),
            vmem((2, GROUP_ROWS, GROUP_SLOTS), BF),
            vmem((2, GROUP_ROWS, GROUP_SLOTS), BF),
            vmem((2, GROUP_SLOTS, HID), BF),
            vmem((2, GROUP_SLOTS, HID), BF),
            vmem((2, GROUP_SLOTS, HID), F32),
            vmem((2, GROUP_SLOTS, HID), F32),
            vmem((ROWS, HALF), F32),
            vmem((2, HALF, HID), BF),
            vmem((2, HALF, HID), BF),
            vmem((HID, HALF), BF),
            vmem((HID, HALF), BF),
            vmem((ROWS, HALF), BF),
            pltpu.SemaphoreType.DMA((8,)),
            pltpu.SemaphoreType.DMA((sems,)),
            pltpu.SemaphoreType.DMA((sems,)),
        ]
    )
    return pl.pallas_call(
        kernel,
        out_shape=jax.ShapeDtypeStruct((ROWS, HALF), BF),
        in_specs=[pl.BlockSpec(memory_space=pl.ANY)] * 6,
        out_specs=pl.BlockSpec(memory_space=pltpu.VMEM),
        scratch_shapes=scratch,
        compiler_params=pltpu.CompilerParams(
            collective_id=0, has_side_effects=True, vmem_limit_bytes=56 << 20
        ),
    )(tokens, expert_ids.T, gate_scores.T, w_gate, w_up, w_down)


def solution(mesh):
    in_specs = (
        P("expert", None),
        P("expert", None),
        P("expert", None),
        P("expert", None, "rep"),
        P("expert", None, "rep"),
        P("expert", "rep", None),
    )
    return jax.shard_map(layer, mesh=mesh, in_specs=in_specs, out_specs=P("expert", "rep"), check_vma=False)
```

time: 53.1 us -> 49.6 us (0.934)
  Pallas kernels: 51.1 us -> 47.5 us
    pallas_call x1, Pallas kernels: 51.1 us -> 47.5 us  [layer(): pl.pallas_call(kernel, out_shape=jax.ShapeDtypeStruct((ROWS, HALF), BF),...]
where the time goes in v4:
time: 49.6 us; the launch traced here: 48.9 us
  Pallas kernels  47.5 us (96%)
  local copies, waits for them, and re-layouts  1.45 us (3%)
    pallas_call x1, Pallas kernels, layer(): pl.pallas_call(kernel, out_shape=jax.ShapeDtypeStruct((ROWS, HALF), BF),...  47.5 us
    unnamed x1, local copies, waits for them, and re-layouts  1.45 us

profile of v4, /device:TPU:32, one launch (start us, length us, event | category | flops | bytes accessed | tf_op | source)
XLA Modules:
  0.0 48.9 jit_solution(4322035258935620933)
XLA Ops:
  0.0 47.5 %shard_map.64 = bf16[16,1792]{1,0:T(8,128)(2,1)} custom-call(bf16[16,3584]{1,0:T(8,128)(2,1)} %tok.1, s32[8,16]{1,0:T(8,128)} %bitcast.2, f32[8,16]{1,0:T(8,128)} %bitcast.3, bf16[1,3584,512]{2,1,0:T(8,128)(2,1)} %wg.1, bf16[1,3584,512]{2,1,0:T(8,128)(2,1)} %wu.1, bf16[1,512,3584]{2,1,0:T(8,128)(2,1)} %wd.1), custom_call_target="tpu_custom_call" | custom-call | tf_op jit(solution)/shard_map/pallas_call | solution.py:301
  47.5 1.4 %copy.8 = bf16[16,1792]{1,0:T(8,128)(2,1)} copy(bf16[16,1792]{1,0:T(8,128)(2,1)} %shard_map.64) | data formatting | bytes 114688

commit v5 on v4

--- a/solution.py
+++ b/solution.py
@@ -15,7 +15,11 @@
 PLANE = NX * NY
 Z_ORDER = (4, 2, 6, 3, 5, 1, 7)
 PLANE_ORDER = (10, 9, 11, 6, 14, 5, 7, 13, 15, 8, 2, 4, 12, 1, 3)
-STEPS = "S00 S01 S10 F00 M00 S11 F01 M01 X00 X01 H00 F10 M10 D00 D01 F11 M11 X10 X11 H10 D10 D11 C00 C01 C10 C11 N00 N01 N10 N11"
+STEPS = (
+    "T00", "S00", "S01", "T10", "S10", "F00", "M00", "S11", "F01", "M01", "X00", "X01",
+    "H00", "F10", "M10", "D00", "D01", "F11", "M11", "X10", "X11", "H10",
+    "D10", "D11", "C00", "C01", "C10", "C11", "N00", "N01", "N10", "N11",
+)
 CHUNKS_IN = ((768, 1024), (1024, 768))
 CHUNKS_OUT = ((1024, 768), (1024, 768))
 GROUPS = ((0, 2, 4, 6), (1, 3, 5, 7))
@@ -148,7 +152,7 @@
     load("wd", wd.at[0, :, pl.ds(pl.multiple_of(mine, 128), HALF)], wd_own)
     push(wd.at[0, :, pl.ds(pl.multiple_of(other, 128), HALF)], wd_sib, "wd", sibling)
     table = meta[...].reshape(NZ * TOP, 128).astype(F32).T
-    for g in range(2):
+    def tables(g, c):
         members, highs, lows = [], [], []
         for p, step in enumerate(GROUPS[g]):
             expert = jnp.where(((lane >> 1) & 3) == p, named, -1.0)
@@ -257,10 +261,10 @@
             out[:, columns] = total.astype(BF)
 
     stages = {
-        "S": select, "F": forward, "M": halves, "X": siblings,
+        "T": tables, "S": select, "F": forward, "M": halves, "X": siblings,
         "H": hidden, "D": down, "C": combine, "N": finish,
     }
-    for name, g, c in STEPS.split():
+    for name, g, c in STEPS:
         stages[name](int(g), int(c))
 
     for ref, key in sent:

time: 49.6 us -> 49.5 us (level)
  no operation moved by 1% of the time
where the time goes in v5:
time: 49.5 us; the launch traced here: 48.8 us
  Pallas kernels  47.4 us (96%)
  local copies, waits for them, and re-layouts  1.45 us (3%)
    pallas_call x1, Pallas kernels, layer(): pl.pallas_call(kernel, out_shape=jax.ShapeDtypeStruct((ROWS, HALF), BF),...  47.4 us
    unnamed x1, local copies, waits for them, and re-layouts  1.45 us

profile of v5, /device:TPU:32, one launch (start us, length us, event | category | flops | bytes accessed | tf_op | source)
XLA Modules:
  0.0 48.8 jit_solution(3765349800705571738)
XLA Ops:
  0.0 47.4 %shard_map.64 = bf16[16,1792]{1,0:T(8,128)(2,1)} custom-call(bf16[16,3584]{1,0:T(8,128)(2,1)} %tok.1, s32[8,16]{1,0:T(8,128)} %bitcast.2, f32[8,16]{1,0:T(8,128)} %bitcast.3, bf16[1,3584,512]{2,1,0:T(8,128)(2,1)} %wg.1, bf16[1,3584,512]{2,1,0:T(8,128)(2,1)} %wu.1, bf16[1,512,3584]{2,1,0:T(8,128)(2,1)} %wd.1), custom_call_target="tpu_custom_call" | custom-call | tf_op jit(solution)/shard_map/pallas_call | solution.py:305
  47.4 1.4 %copy.8 = bf16[16,1792]{1,0:T(8,128)(2,1)} copy(bf16[16,1792]{1,0:T(8,128)(2,1)} %shard_map.64) | data formatting | bytes 114688
